TPU v7x, 512 devices: a whole 4x8x8 slice. The times are simulated.
512 devices in a mesh: seq: 128 (over y, z, core), fsdp: 4 (over x).
Axes of the slice: x: 4, y: 8, z: 8, core: 2. Of those that a mesh axis runs over, the one named last changes fastest.
Arguments:
- tokens: bfloat16 [4, 16384, 2048], P('fsdp', 'seq'), may hold values from -14 to 14
- w_qkv: bfloat16 [2048, 3, 1024], P(None, None, 'fsdp'), may hold values from -0.125 to 0.125
- w_feature: bfloat16 [8, 128, 16], replicated, may hold values from -2 to 2
- norm_gain: float32 [1024], replicated, may hold values from 0.5 to 1.5
- log_decay: float32 [4, 8, 16384], P('fsdp', None, 'seq'), may hold values from -1.5 to 0
- pattern: int32 [4, 256, 3], P('fsdp', 'seq'), may hold values from 1 to 255, as said below
Outputs:
- mixed: bfloat16 [4, 16384, 1024], P('fsdp', 'seq')
Inputs may be any that keep to these rules, and one draw needn't show every extreme that they name: `pattern`: the 3 blocks of query block b are distinct, none is among the first 1 block or equal to b - 1, b or b + 1, and each lies in a segment at most 3 segments from b's segment; the first lies exactly 3 segments later where that segment exists, else 3 segments earlier.
All inputs are finite; a program needn't handle non-finite values.
Results may differ from a plain program's by a relative error of at most 0.0097.
The roundings to bfloat16 on the way count: a program that leaves them out, or rounds other values in their place, can miss the bound.
Values may be sent and summed in bfloat16 or wider, within the bound.
No kernel may reach another device: no remote copies, remote signals or barrier semaphores. Data moves between devices by JAX's collectives and lax.ppermute only.
A program may use at most 64 MiB of HBM per device.

v0:
```python
import jax
import jax.numpy as jnp
from jax import lax
from jax.sharding import PartitionSpec as P

HALF_HEADS = 8
DH = 128
F = 16
HD = 1024
BS = 64
G = 1
R = 3
RD = 3
TOK_DEV = 128
NB_DEV = 2
epsilon = 1e-06
masked_score = -1e30


def from_behind(value, axis, steps):
    count = lax.axis_size(axis)
    initial, last = (max(0, -steps), min(count, count - steps))
    return lax.ppermute(value, axis, [(source, source + steps) for source in range(initial, last)])


def spread(array, axis, root):
    mine = lax.axis_index(axis) == root
    return lax.psum(jnp.where(mine, array, jnp.zeros_like(array)), axis)


def entering(value, axis, join, neutral):
    count, mine = (lax.axis_size(axis), lax.axis_index(axis))
    pieces = jax.tree.map(lambda part: lax.all_gather(part, axis), value)
    running = jax.tree.map(
        lambda part, zero: jnp.full_like(part, 0) + jnp.asarray(zero, part.dtype), value, neutral
    )

    def lap(position, running):
        longer = join(running, jax.tree.map(lambda part: part[position], pieces))
        return jax.tree.map(lambda new, old: jnp.where(position < mine, new, old), longer, running)

    return lax.fori_loop(0, count - 1, lap, running)


def feature_map(projected_head, w_feature):
    logits = jnp.einsum(
        "thd,hdf->htf", projected_head, w_feature, preferred_element_type=jnp.float32
    )
    return jax.nn.softmax(logits, axis=-1).astype(jnp.bfloat16)


def combine_states(earlier, following):
    return (earlier[0] * following[0], following[0][:, None, None] * earlier[1] + following[1])


def neighbour_piece(pair_rows, offset):
    return from_behind(pair_rows, "seq", -offset)


def per_device(tokens, w_qkv, w_feature, norm_gain, log_decay, pattern):
    projected = jnp.einsum(
        "btd,dkc->btkc",
        tokens,
        lax.all_gather(w_qkv, "fsdp", axis=2, tiled=True),
        preferred_element_type=jnp.float32,
    ).astype(jnp.bfloat16)
    queries = projected[0, :, 0].reshape(TOK_DEV, HALF_HEADS, DH)
    key_rows = projected[0, :, 1].reshape(TOK_DEV, HALF_HEADS, DH)
    values = projected[0, :, 2].reshape(TOK_DEV, HALF_HEADS, DH)
    pair_rows = projected[:, :, 1:3].reshape(1, TOK_DEV, 2 * HD)
    pieces = []
    for offset in range(-RD, RD + 1):
        if offset == 0:
            pieces.append(pair_rows)
        else:
            pieces.append(neighbour_piece(pair_rows, offset))
    region = jnp.concatenate(pieces, axis=1)
    global_rows = spread(pair_rows[0, : G * BS], "seq", 0)
    phi_query = feature_map(queries, w_feature)
    phi_key = feature_map(key_rows, w_feature)
    log_steps = log_decay[0]
    cumulative = jnp.cumsum(log_steps, axis=1)
    final_log = cumulative[:, -1:]
    weighted_key = (
        jnp.exp(final_log - cumulative)[:, :, None] * phi_key.astype(jnp.float32)
    ).astype(jnp.bfloat16)
    local_state = jnp.einsum(
        "htf,thd->hfd", weighted_key, values, preferred_element_type=jnp.float32
    )
    identity = (jnp.ones((HALF_HEADS,), jnp.float32), jnp.zeros((HALF_HEADS, F, DH), jnp.float32))
    carried_pair = entering(
        (jnp.exp(final_log[:, 0]), local_state), "seq", combine_states, identity
    )
    carried = carried_pair[1]
    scores = jnp.einsum("htf,hsf->hts", phi_query, phi_key, preferred_element_type=jnp.float32)
    log_gap = cumulative[:, :, None] - cumulative[:, None, :]
    causal = jnp.arange(TOK_DEV)[:, None] >= jnp.arange(TOK_DEV)[None, :]
    decay_matrix = jnp.where(causal[None], jnp.exp(jnp.minimum(log_gap, 0.0)), 0.0)
    mixing = (scores * decay_matrix).astype(jnp.bfloat16)
    local_term = jnp.einsum("hts,shd->thd", mixing, values, preferred_element_type=jnp.float32)
    carried_term = jnp.einsum(
        "htf,hfd->thd", phi_query.astype(jnp.float32), carried, precision=lax.Precision.HIGHEST
    )
    carried_term = carried_term * jnp.exp(cumulative).T[:, :, None]
    linear = local_term + carried_term
    normed = linear * lax.rsqrt(jnp.mean(linear * linear, axis=-1, keepdims=True) + epsilon)
    normed = normed * norm_gain.reshape(HALF_HEADS, DH)
    device = lax.axis_index("seq")
    block_total = lax.axis_size("seq") * NB_DEV
    window_blocks = region[0].reshape((2 * RD + 1) * NB_DEV, BS, 2 * HD)
    query_blocks = device * NB_DEV + jnp.arange(NB_DEV, dtype=jnp.int32)
    near_blocks = query_blocks[:, None] + jnp.arange(-1, 2, dtype=jnp.int32)[None, :]
    usable_near = (near_blocks >= G) & (near_blocks < block_total)
    chosen = jnp.concatenate([near_blocks, pattern[0]], axis=1) - (device - RD) * NB_DEV
    chosen = jnp.clip(chosen, 0, (2 * RD + 1) * NB_DEV - 1)
    usable = jnp.concatenate([usable_near, jnp.ones((NB_DEV, R), dtype=bool)], axis=1)
    usable_keys = jnp.repeat(usable, BS, axis=1)
    picked = jnp.take(window_blocks, chosen, axis=0).reshape(
        NB_DEV, (3 + R) * BS, 2, HALF_HEADS, DH
    )
    global_split = global_rows.reshape(G * BS, 2, HALF_HEADS, DH)
    query_rows = queries.reshape(NB_DEV, BS, HALF_HEADS, DH)
    score_scale = DH ** (-0.5)
    near_scores = (
        jnp.einsum(
            "nqhd,nkhd->nhqk", query_rows, picked[:, :, 0], preferred_element_type=jnp.float32
        )
        * score_scale
    )
    near_scores = jnp.where(usable_keys[:, None, None, :], near_scores, masked_score)
    far_scores = (
        jnp.einsum(
            "nqhd,khd->nhqk", query_rows, global_split[:, 0], preferred_element_type=jnp.float32
        )
        * score_scale
    )
    scores_all = jnp.concatenate([near_scores, far_scores], axis=-1)
    highest = jnp.max(scores_all, axis=-1, keepdims=True)
    exponent = jnp.exp(scores_all - highest)
    denominator = jnp.sum(exponent, axis=-1, keepdims=True)
    soft_weights = (exponent / denominator).astype(jnp.bfloat16)
    near_count = (3 + R) * BS
    sparse = jnp.einsum(
        "nhqk,nkhd->nqhd",
        soft_weights[..., :near_count],
        picked[:, :, 1],
        preferred_element_type=jnp.float32,
    )
    sparse = sparse + jnp.einsum(
        "nhqk,khd->nqhd",
        soft_weights[..., near_count:],
        global_split[:, 1],
        preferred_element_type=jnp.float32,
    )
    sparse = sparse.reshape(TOK_DEV, HALF_HEADS, DH)
    return (normed + sparse).astype(jnp.bfloat16).reshape(1, TOK_DEV, HD)


def solution(mesh):
    placed = (
        P("fsdp", "seq", None),
        P(None, None, "fsdp"),
        P(),
        P(),
        P("fsdp", None, "seq"),
        P("fsdp", "seq", None),
    )
    return jax.shard_map(
        per_device, mesh=mesh, in_specs=placed, out_specs=P("fsdp", "seq", None), check_vma=False
    )
```

profile of v0, /device:TPU:9, one launch (start us, length us, event | category | flops | bytes accessed | tf_op | source)
XLA Modules:
  0.0 615.5 jit_solution(8857086100503208488)
XLA Ops:
  7.9 133.5 %all-gather.5.cloned.1.call-done = bf16[2048,3,1024]{2,0,1:T(8,128)(2,1)} async-done(((bf16[2048,3,256]{2,0,1:T(8,128)(2,1)}), bf16[2048,3,1024]{2,0,1:T(8,128)(2,1)}) %all-gather.5.cloned.1.call-update) | async-done | bytes 12582928 | tf_op jit(solution)/shard_map/all_gather | solution.py:64
  141.4 6.4 %fusion.7 = bf16[1,128,3,1024]{3,1,2,0:T(8,128)(2,1)S(1)} fusion(bf16[2048,3,1024]{2,0,1:T(8,128)(2,1)} %all-gather.5.cloned.1.call-done, bf16[1,128,2048]{2,1,0:T(8,128)(2,1)S(1)} %copy-done), kind=kOutput, calls=%fused_computation.17 | convolution fusion | flops 1611005952 | bytes 13893632 | tf_op jit(solution)/shard_map/btd,dkc->btkc/dot_general | solution.py:61
  151.9 1.3 dynamic-slice
  154.0 213.7 %all-reduce.1 = f32[1024]{0:T(1024)S(1)} all-reduce(f32[1024]{0:T(1024)S(1)} %dynamic-update-slice), channel_id=2, replica_groups=mesh['seq'=128,'fsdp'=4] {'seq'}, use_global_device_ids=true, to_apply=%add.1 | all-reduce | flops 1024 | bytes 8192
  368.4 1.9 collective-permute-start
  370.3 1.9 collective-permute-start.1
  372.3 2.1 collective-permute-start.2
  374.3 5.9 collective-permute-start.3
  380.2 7.2 %collective-permute-start.4 = (bf16[1,128,2048]{1,2,0:T(8,128)(2,1)S(1)}, bf16[1,128,2048]{1,2,0:T(8,128)(2,1)S(1)}, u32[]{:S(2)}, u32[]{:S(2)}) collective-permute-start(bf16[1,128,2048]{1,2,0:T(8,128)(2,1)S(1)} %bitcast.123), channel_id=1, source_target_pairs={{8,0},{12,4},{16,8},{20,12},{24,16},{28,20},{32,24},{36,28},{40,32... | collective-permute-start | bytes 1572872 | tf_op jit(solution)/shard_map/ppermute | solution.py:23
  388.0 1.1 fusion.37
  389.4 8.5 %collective-permute-done = bf16[1,128,2048]{1,2,0:T(8,128)(2,1)} collective-permute-done((bf16[1,128,2048]{1,2,0:T(8,128)(2,1)S(1)}, bf16[1,128,2048]{1,2,0:T(8,128)(2,1)}, u32[]{:S(2)}, u32[]{:S(2)}) %collective-permute-start) | collective-permute-done | bytes 524320 | tf_op jit(solution)/shard_map/ppermute | solution.py:23
  397.9 3.3 collective-permute-start.5
  401.2 1.9 constant_dynamic-update-slice_fusion.6
  403.1 1.9 constant_dynamic-update-slice_fusion.5
  405.4 1.9 constant_dynamic-update-slice_fusion.4
  408.2 1.0 constant_dynamic-update-slice_fusion.2
  410.1 3.3 collective-permute-done.5
  414.2 6.2 %copy.54 = bf16[1,896,2048]{2,1,0:T(8,128)(2,1)} copy(bf16[1,896,2048]{1,2,0:T(8,128)(2,1)} %constant_dynamic-update-slice_fusion) | data formatting | bytes 7340032 | tf_op jit(solution)/shard_map/concatenate | solution.py:77
  420.4 4.6 gather_fusion
  425.0 2.9 copy.70
  432.0 52.2 %all-gather.7.cloned.1.call-done = f32[1024,16,128]{2,1,0:T(8,128)} async-done(((f32[8,16,128]{2,1,0:T(8,128)}), f32[1024,16,128]{2,1,0:T(8,128)}) %all-gather.7.cloned.1.call-update) | async-done | bytes 8388624 | tf_op jit(solution)/shard_map/all_gather | solution.py:33
  484.2 122.4 %while.14 = (s32[]{:T(128)}, f32[8,16,128]{2,1,0:T(8,128)S(1)}, s32[]{:T(128)}, f32[128,8]{1,0:T(8,128)S(1)}, f32[128,8,16,128]{3,2,1,0:T(8,128)}, /*index=5*/s32[]{:T(128)}, s32[]{:T(128)}) while((s32[]{:T(128)}, f32[8,16,128]{2,1,0:T(8,128)S(1)}, s32[]{:T(128)}, f32[128,8]{1,0:T(8,128)S(1)}, f32[128,8,16,128]{3,2,1,0:T(8,128)}, ...), condition=%wide.region_6.7_spmd.clone, body=%wide.region_5.6_spmd.clone.sunk | while | flops 65540 | bytes 196809 | solution.py:42
  485.2 0.9 fusion.58
  486.1 0.9 fusion.58
  487.1 0.9 fusion.58
  488.1 0.9 fusion.58
  489.0 0.9 fusion.58
  491.0 0.9 fusion.58
  492.9 0.9 fusion.58
  493.8 0.9 fusion.58
  494.8 0.9 fusion.58
  495.8 0.9 fusion.58
  (333 shorter events, 125.5 us)
Async XLA Ops:
  6.5 134.9 %copy-start = (bf16[1,128,2048]{2,1,0:T(8,128)(2,1)S(1)}, bf16[1,128,2048]{2,1,0:T(8,128)(2,1)}, u32[]{:S(2)}) copy-start(bf16[1,128,2048]{2,1,0:T(8,128)(2,1)} %param.8) | copy-start | bytes 1572868
  6.5 0.8 copy-start.6
  6.5 134.9 %all-gather.5.cloned.1.call-start = ((), (), s32[]{:S(2)}) async-start(), calls=%async_computation | async-start | bytes 15728640 | tf_op jit(solution)/shard_map/all_gather | solution.py:64
  7.3 380.8 %all-reduce.4.cloned.1.call-start = ((), (), s32[]{:S(2)}) async-start(), calls=%async_computation.1 | async-start | bytes 524288 | tf_op jit(solution)/shard_map/psum | solution.py:28
  147.8 1.5 copy-start.7
  147.8 2.8 copy-start.5
  149.2 335.0 %all-gather.7.cloned.1.call-start = ((), (), s32[]{:S(2)}) async-start(), calls=%async_computation.2 | async-start | bytes 8454144 | tf_op jit(solution)/shard_map/all_gather | solution.py:33
  149.5 237.9 %copy-start.8 = (f32[8,128,16]{1,2,0:T(8,128)}, f32[8,128,16]{1,2,0:T(8,128)S(1)}, u32[]{:S(2)}) copy-start(f32[8,128,16]{1,2,0:T(8,128)S(1)} %fusion.26) | copy-start | bytes 196612
  149.6 0.9 copy-start.10
  368.4 29.5 %collective-permute-start = (bf16[1,128,2048]{1,2,0:T(8,128)(2,1)S(1)}, bf16[1,128,2048]{1,2,0:T(8,128)(2,1)}, u32[]{:S(2)}, u32[]{:S(2)}) collective-permute-start(bf16[1,128,2048]{1,2,0:T(8,128)(2,1)S(1)} %bitcast.119), channel_id=1, source_target_pairs={{0,12},{4,16},{8,20},{12,24},{16,28},{20,32},{24,36},{28,40},{32,4... | collective-permute-start | bytes 1572872 | tf_op jit(solution)/shard_map/ppermute | solution.py:23
  370.3 32.8 %collective-permute-start.1 = (bf16[1,128,2048]{1,2,0:T(8,128)(2,1)S(1)}, bf16[1,128,2048]{1,2,0:T(8,128)(2,1)}, u32[]{:S(2)}, u32[]{:S(2)}) collective-permute-start(bf16[1,128,2048]{1,2,0:T(8,128)(2,1)S(1)} %bitcast.120), channel_id=1, source_target_pairs={{0,8},{4,12},{8,16},{12,20},{16,24},{20,28},{24,32},{28,36},{32,40... | collective-permute-start | bytes 1572872 | tf_op jit(solution)/shard_map/ppermute | solution.py:23
  372.3 33.1 %collective-permute-start.2 = (bf16[1,128,2048]{1,2,0:T(8,128)(2,1)S(1)}, bf16[1,128,2048]{1,2,0:T(8,128)(2,1)}, u32[]{:S(2)}, u32[]{:S(2)}) collective-permute-start(bf16[1,128,2048]{1,2,0:T(8,128)(2,1)S(1)} %bitcast.121), channel_id=1, source_target_pairs={{0,4},{4,8},{8,12},{12,16},{16,20},{20,24},{24,28},{28,32},{32,36}... | collective-permute-start | bytes 1572872 | tf_op jit(solution)/shard_map/ppermute | solution.py:23
  374.3 33.8 %collective-permute-start.3 = (bf16[1,128,2048]{1,2,0:T(8,128)(2,1)S(1)}, bf16[1,128,2048]{1,2,0:T(8,128)(2,1)S(1)}, u32[]{:S(2)}, u32[]{:S(2)}) collective-permute-start(bf16[1,128,2048]{1,2,0:T(8,128)(2,1)S(1)} %bitcast.122), channel_id=1, source_target_pairs={{4,0},{8,4},{12,8},{16,12},{20,16},{24,20},{28,24},{32,28},{36,32}... | collective-permute-start | bytes 1572872 | tf_op jit(solution)/shard_map/ppermute | solution.py:23
  380.2 28.9 %collective-permute-start.4 = (bf16[1,128,2048]{1,2,0:T(8,128)(2,1)S(1)}, bf16[1,128,2048]{1,2,0:T(8,128)(2,1)S(1)}, u32[]{:S(2)}, u32[]{:S(2)}) collective-permute-start(bf16[1,128,2048]{1,2,0:T(8,128)(2,1)S(1)} %bitcast.123), channel_id=1, source_target_pairs={{8,0},{12,4},{16,8},{20,12},{24,16},{28,20},{32,24},{36,28},{40,32... | collective-permute-start | bytes 1572872 | tf_op jit(solution)/shard_map/ppermute | solution.py:23
  397.9 15.4 %collective-permute-start.5 = (bf16[1,128,2048]{1,2,0:T(8,128)(2,1)S(1)}, bf16[1,128,2048]{1,2,0:T(8,128)(2,1)S(1)}, u32[]{:S(2)}, u32[]{:S(2)}) collective-permute-start(bf16[1,128,2048]{1,2,0:T(8,128)(2,1)S(1)} %bitcast.124), channel_id=1, source_target_pairs={{12,0},{16,4},{20,8},{24,12},{28,16},{32,20},{36,24},{40,28},{44,3... | collective-permute-start | bytes 1572872 | tf_op jit(solution)/shard_map/ppermute | solution.py:23
  427.9 0.8 copy-start.3
  430.3 1.0 copy-start.1
  431.2 176.0 %copy-start.2 = (pred[128,128]{1,0:T(8,128)(4,1)S(1)}, pred[128,128]{1,0:T(8,128)(4,1)}, u32[]{:S(2)}) copy-start(pred[128,128]{1,0:T(8,128)(4,1)} %iota_compare_fusion) | copy-start | bytes 49156
  431.3 176.0 %copy-start.9 = (f32[8,128,16]{1,2,0:T(8,128)S(1)}, f32[8,128,16]{1,2,0:T(8,128)}, u32[]{:S(2)}) copy-start(f32[8,128,16]{1,2,0:T(8,128)} %copy-done.8) | copy-start | bytes 196612
  431.3 176.0 %copy-start.11 = (f32[8,128]{1,0:T(8,128)S(1)}, f32[8,128]{1,0:T(8,128)}, u32[]{:S(2)}) copy-start(f32[8,128]{1,0:T(8,128)} %copy-done.10) | copy-start | bytes 12292
  431.5 176.4 %copy-start.4 = (f32[1024]{0:T(1024)S(1)}, f32[1024]{0:T(1024)}, u32[]{:S(2)}) copy-start(f32[1024]{0:T(1024)} %param.11) | copy-start | bytes 12292
Sparse Core Ops, SparseCore 0:
  9.5 131.8 all-gather.4
  149.3 190.4 all-reduce.3
  342.9 141.2 all-gather.6
where the time goes:
time: 622 us; the launch traced here: 615 us
  blocking collectives  214 us (34%)
  waiting for transfers between devices  199 us (32%)
  other arithmetic  121 us (19%)
  local copies, waits for them, and re-layouts  30.1 us (5%)
  starting transfers between devices  22.4 us (4%)
  between operations  14.2 us (2%)
  matrix products  11.5 us (2%)
    unnamed x1, blocking collectives  214 us
    all_gather x1, waiting for transfers between devices, per_device(): lax.all_gather(w_qkv, 'fsdp', axis=2, tiled=True)  134 us
    select_n x127, other arithmetic, lap(): jnp.where(position < mine, new, old)  117 us
    all_gather x1, waiting for transfers between devices, entering(): pieces = jax.tree.map(lambda part: lax.all_gather(part, axis), value)  52.2 us
    ppermute x6, starting transfers between devices, from_behind(): lax.ppermute(value, axis, [(source, source + steps) for source in range(i...  22.3 us
    unnamed x38, local copies, waits for them, and re-layouts  13.2 us
  transfers between devices with their start and end apart: 9, of which 5 were waited for; matrix products, arithmetic and copies ran while one was open for 6% of the time, Pallas kernels for 0%

commit v1 on v0

--- a/solution.py
+++ b/solution.py
@@ -15,6 +15,19 @@
 NB_DEV = 2
 epsilon = 1e-06
 masked_score = -1e30
+
+
+def gather_around(shard, axis, dim):
+    ways = lax.axis_size(axis)
+    up = [(d, (d + 1) % ways) for d in range(ways)]
+    down = [(d, (d - 1) % ways) for d in range(ways)]
+    earlier, later = ([shard], [shard])
+    for _ in range(ways // 2):
+        earlier.append(lax.ppermute(earlier[-1], axis, up))
+    for _ in range((ways - 1) // 2):
+        later.append(lax.ppermute(later[-1], axis, down))
+    line = jnp.concatenate([*earlier[::-1], *later[1:]], axis=dim)
+    return jnp.roll(line, (lax.axis_index(axis) - ways // 2) * shard.shape[dim], axis=dim)
 
 
 def from_behind(value, axis, steps):
@@ -59,10 +72,7 @@
 
 def per_device(tokens, w_qkv, w_feature, norm_gain, log_decay, pattern):
     projected = jnp.einsum(
-        "btd,dkc->btkc",
-        tokens,
-        lax.all_gather(w_qkv, "fsdp", axis=2, tiled=True),
-        preferred_element_type=jnp.float32,
+        "btd,dkc->btkc", tokens, gather_around(w_qkv, "fsdp", 2), preferred_element_type=jnp.float32
     ).astype(jnp.bfloat16)
     queries = projected[0, :, 0].reshape(TOK_DEV, HALF_HEADS, DH)
     key_rows = projected[0, :, 1].reshape(TOK_DEV, HALF_HEADS, DH)

time: 622 us -> 739 us (1.19)
  the two profiles are of different devices: /device:TPU:9 before, /device:TPU:1 now
where the time goes in v1:
time: 739 us; the launch traced here: 728 us
  blocking collectives  258 us (35%)
  waiting for transfers between devices  165 us (22%)
  local copies, waits for them, and re-layouts  129 us (17%)
  other arithmetic  122 us (17%)
  starting transfers between devices  27.6 us (4%)
  between operations  14.6 us (2%)
  matrix products  9.19 us (1%)
    unnamed x1, blocking collectives  258 us
    ppermute x2, waiting for transfers between devices, gather_around(): earlier.append(lax.ppermute(earlier[-1], axis, up))  127 us
    select_n x127, other arithmetic, lap(): jnp.where(position < mine, new, old)  117 us
    mul x127, local copies, waits for them, and re-layouts, combine_states(): following[0][:, None, None] * earlier[1] + following[1]  87.2 us
    unnamed x58, local copies, waits for them, and re-layouts  28.4 us
    all_gather x1, waiting for transfers between devices, entering(): pieces = jax.tree.map(lambda part: lax.all_gather(part, axis), value)  21.2 us
    ppermute x6, waiting for transfers between devices, from_behind(): lax.ppermute(value, axis, [(source, source + steps) for source in range(i...  17.5 us
  transfers between devices with their start and end apart: 11, of which 6 were waited for; matrix products, arithmetic and copies ran while one was open for 5% of the time, Pallas kernels for 0%

profile of v1, /device:TPU:1, one launch (start us, length us, event | category | flops | bytes accessed | tf_op | source)
XLA Modules:
  0.0 728.1 jit_solution(8804246705211678694)
XLA Ops:
  6.5 4.8 copy.47
  11.3 3.9 collective-permute-start
  15.2 63.5 %collective-permute-done = bf16[2048,3,256]{0,2,1:T(8,128)(2,1)} collective-permute-done((bf16[2048,3,256]{0,2,1:T(8,128)(2,1)}, bf16[2048,3,256]{0,2,1:T(8,128)(2,1)}, u32[]{:S(2)}, u32[]{:S(2)}) %collective-permute-start) | collective-permute-done | bytes 3145760 | tf_op jit(solution)/shard_map/ppermute | solution.py:26
  78.7 6.7 collective-permute-start.1
  85.4 4.2 collective-permute-start.2
  90.2 63.2 %collective-permute-done.1 = bf16[2048,3,256]{0,2,1:T(8,128)(2,1)} collective-permute-done((bf16[2048,3,256]{0,2,1:T(8,128)(2,1)}, bf16[2048,3,256]{0,2,1:T(8,128)(2,1)}, u32[]{:S(2)}, u32[]{:S(2)}) %collective-permute-start.1) | collective-permute-done | bytes 3145760 | tf_op jit(solution)/shard_map/ppermute | solution.py:26
  153.4 2.3 constant_dynamic-update-slice_fusion.7
  155.7 2.4 constant_dynamic-update-slice_fusion.6
  158.9 2.3 constant_dynamic-update-slice_fusion.4
  161.2 2.3 constant_dynamic-update-slice_fusion.3
  163.5 2.3 constant_dynamic-update-slice_fusion.2
  166.2 2.3 constant_dynamic-update-slice_fusion
  168.6 3.5 fusion.12
  176.4 1.2 dynamic-slice
  178.4 258.2 %all-reduce.1 = f32[1024]{0:T(1024)S(1)} all-reduce(f32[1024]{0:T(1024)S(1)} %dynamic-update-slice), channel_id=2, replica_groups=mesh['seq'=128,'fsdp'=4] {'seq'}, use_global_device_ids=true, to_apply=%add.1 | all-reduce | flops 1024 | bytes 8192
  438.6 2.1 collective-permute-start.3
  440.7 1.3 collective-permute-start.4
  442.0 1.9 collective-permute-start.5
  443.9 4.6 collective-permute-start.6
  448.5 1.3 collective-permute-start.7
  450.1 0.9 fusion.50
  451.0 1.2 fusion.49
  452.3 1.1 fusion.38
  453.7 1.5 collective-permute-start.8
  455.2 1.9 constant_dynamic-update-slice_fusion.14
  457.1 2.3 collective-permute-done.4
  460.3 8.2 %collective-permute-done.5 = bf16[1,128,2048]{2,1,0:T(8,128)(2,1)S(1)} collective-permute-done((bf16[1,128,2048]{2,1,0:T(8,128)(2,1)S(1)}, bf16[1,128,2048]{2,1,0:T(8,128)(2,1)S(1)}, u32[]{:S(2)}, u32[]{:S(2)}) %collective-permute-start.5) | collective-permute-done | bytes 524320 | tf_op jit(solution)/shard_map/ppermute | solution.py:36
  471.9 7.1 collective-permute-done.8
  479.8 4.7 gather_fusion
  484.5 3.0 copy.75
  491.6 21.2 %all-gather.4.cloned.1.call-done = f32[1024,16,128]{2,1,0:T(8,128)} async-done(((f32[8,16,128]{2,1,0:T(8,128)}), f32[1024,16,128]{2,1,0:T(8,128)}) %all-gather.4.cloned.1.call-update) | async-done | bytes 8388624 | tf_op jit(solution)/shard_map/all_gather | solution.py:46
  512.8 206.2 %while.14 = (s32[]{:T(128)}, f32[8,16,128]{2,1,0:T(8,128)S(1)}, s32[]{:T(128)}, f32[128,8]{1,0:T(8,128)}, f32[128,8,16,128]{3,2,1,0:T(8,128)}, /*index=5*/s32[]{:T(128)}, s32[]{:T(128)}) while((s32[]{:T(128)}, f32[8,16,128]{2,1,0:T(8,128)S(1)}, s32[]{:T(128)}, f32[128,8]{1,0:T(8,128)}, f32[128,8,16,128]{3,2,1,0:T(8,128)}, ...), condition=%wide.region_6.7_spmd.clone, body=%wide.region_5.6_spmd.clone.sunk | while | flops 65540 | bytes 196817 | solution.py:55
  (358 shorter events, 223.7 us)
Async XLA Ops:
  6.5 162.0 %copy-start = (bf16[1,128,2048]{2,1,0:T(8,128)(2,1)S(1)}, bf16[1,128,2048]{2,1,0:T(8,128)(2,1)}, u32[]{:S(2)}) copy-start(bf16[1,128,2048]{2,1,0:T(8,128)(2,1)} %param.8) | copy-start | bytes 1572868
  6.5 83.1 %copy-start.16 = (f32[1,8,128]{2,1,0:T(8,128)S(1)}, f32[1,8,128]{2,1,0:T(8,128)}, u32[]{:S(2)}) copy-start(f32[1,8,128]{2,1,0:T(8,128)} %param.12) | copy-start | bytes 12292
  6.5 445.8 %all-reduce.4.cloned.1.call-start = ((), (), s32[]{:S(2)}) async-start(), calls=%async_computation | async-start | bytes 524288 | tf_op jit(solution)/shard_map/psum | solution.py:41
  11.3 67.4 %collective-permute-start = (bf16[2048,3,256]{0,2,1:T(8,128)(2,1)}, bf16[2048,3,256]{0,2,1:T(8,128)(2,1)}, u32[]{:S(2)}, u32[]{:S(2)}) collective-permute-start(bf16[2048,3,256]{0,2,1:T(8,128)(2,1)} %copy.47), channel_id=1, source_target_pairs={{0,1},{1,2},{2,3},{3,0},{4,5},{5,6},{6,7},{7,4},{8,9},{9,10},{10,1... | collective-permute-start | bytes 9437192 | tf_op jit(solution)/shard_map/ppermute | solution.py:26
  78.7 74.6 %collective-permute-start.1 = (bf16[2048,3,256]{0,2,1:T(8,128)(2,1)}, bf16[2048,3,256]{0,2,1:T(8,128)(2,1)}, u32[]{:S(2)}, u32[]{:S(2)}) collective-permute-start(bf16[2048,3,256]{0,2,1:T(8,128)(2,1)} %collective-permute-done), channel_id=1, source_target_pairs={{0,1},{1,2},{2,3},{3,0},{4,5},{5,6},{6,7},{7,4},{8,9},{9,10},{10,1... | collective-permute-start | bytes 9437192 | tf_op jit(solution)/shard_map/ppermute | solution.py:26
  85.4 73.5 %collective-permute-start.2 = (bf16[2048,3,256]{0,2,1:T(8,128)(2,1)}, bf16[2048,3,256]{0,2,1:T(8,128)(2,1)}, u32[]{:S(2)}, u32[]{:S(2)}) collective-permute-start(bf16[2048,3,256]{0,2,1:T(8,128)(2,1)} %copy.47), channel_id=1, source_target_pairs={{0,3},{1,0},{2,1},{3,2},{4,7},{5,4},{6,5},{7,6},{8,11},{9,8},{10,9... | collective-permute-start | bytes 9437192 | tf_op jit(solution)/shard_map/ppermute | solution.py:28
  155.7 2.8 copy-start.2
  172.0 1.3 copy-start.7
  172.0 2.5 copy-start.15
  172.1 271.8 %copy-start.3 = (bf16[1,128,1,1024]{1,3,2,0:T(8,128)(2,1)}, bf16[1,128,1,1024]{1,3,2,0:T(8,128)(2,1)S(1)}, u32[]{:S(2)}) copy-start(bf16[1,128,1,1024]{1,3,2,0:T(8,128)(2,1)S(1)} %get-tuple-element.132) | copy-start | bytes 786436
  173.2 339.6 %all-gather.4.cloned.1.call-start = ((), (), s32[]{:S(2)}) async-start(), calls=%async_computation.1 | async-start | bytes 8454144 | tf_op jit(solution)/shard_map/all_gather | solution.py:46
  173.5 276.4 %copy-start.8 = (f32[8,128,16]{1,2,0:T(8,128)}, f32[8,128,16]{1,2,0:T(8,128)S(1)}, u32[]{:S(2)}) copy-start(f32[8,128,16]{1,2,0:T(8,128)S(1)} %fusion.51) | copy-start | bytes 196612
  173.5 0.9 copy-start.17
  438.6 15.1 %collective-permute-start.3 = (bf16[1,128,2048]{2,1,0:T(8,128)(2,1)S(1)}, bf16[1,128,2048]{2,1,0:T(8,128)(2,1)}, u32[]{:S(2)}, u32[]{:S(2)}) collective-permute-start(bf16[1,128,2048]{2,1,0:T(8,128)(2,1)S(1)} %copy.54), channel_id=1, source_target_pairs={{0,12},{4,16},{8,20},{12,24},{16,28},{20,32},{24,36},{28,40},{32,4... | collective-permute-start | bytes 1572872 | tf_op jit(solution)/shard_map/ppermute | solution.py:36
  440.7 18.7 %collective-permute-start.4 = (bf16[1,128,2048]{2,1,0:T(8,128)(2,1)S(1)}, bf16[1,128,2048]{2,1,0:T(8,128)(2,1)S(1)}, u32[]{:S(2)}, u32[]{:S(2)}) collective-permute-start(bf16[1,128,2048]{2,1,0:T(8,128)(2,1)S(1)} %copy.54), channel_id=1, source_target_pairs={{0,8},{4,12},{8,16},{12,20},{16,24},{20,28},{24,32},{28,36},{32,40... | collective-permute-start | bytes 1572872 | tf_op jit(solution)/shard_map/ppermute | solution.py:36
  442.0 26.5 %collective-permute-start.5 = (bf16[1,128,2048]{2,1,0:T(8,128)(2,1)S(1)}, bf16[1,128,2048]{2,1,0:T(8,128)(2,1)S(1)}, u32[]{:S(2)}, u32[]{:S(2)}) collective-permute-start(bf16[1,128,2048]{2,1,0:T(8,128)(2,1)S(1)} %copy.54), channel_id=1, source_target_pairs={{0,4},{4,8},{8,12},{12,16},{16,20},{20,24},{24,28},{28,32},{32,36}... | collective-permute-start | bytes 1572872 | tf_op jit(solution)/shard_map/ppermute | solution.py:36
  443.9 26.2 %collective-permute-start.6 = (bf16[1,128,2048]{2,1,0:T(8,128)(2,1)S(1)}, bf16[1,128,2048]{2,1,0:T(8,128)(2,1)S(1)}, u32[]{:S(2)}, u32[]{:S(2)}) collective-permute-start(bf16[1,128,2048]{2,1,0:T(8,128)(2,1)S(1)} %copy.54), channel_id=1, source_target_pairs={{4,0},{8,4},{12,8},{16,12},{20,16},{24,20},{28,24},{32,28},{36,32}... | collective-permute-start | bytes 1572872 | tf_op jit(solution)/shard_map/ppermute | solution.py:36
  448.5 22.5 %collective-permute-start.7 = (bf16[1,128,2048]{2,1,0:T(8,128)(2,1)S(1)}, bf16[1,128,2048]{2,1,0:T(8,128)(2,1)S(1)}, u32[]{:S(2)}, u32[]{:S(2)}) collective-permute-start(bf16[1,128,2048]{2,1,0:T(8,128)(2,1)S(1)} %copy.54), channel_id=1, source_target_pairs={{8,0},{12,4},{16,8},{20,12},{24,16},{28,20},{32,24},{36,28},{40,32... | collective-permute-start | bytes 1572872 | tf_op jit(solution)/shard_map/ppermute | solution.py:36
  453.7 25.2 %collective-permute-start.8 = (bf16[1,128,2048]{2,1,0:T(8,128)(2,1)S(1)}, bf16[1,128,2048]{2,1,0:T(8,128)(2,1)S(1)}, u32[]{:S(2)}, u32[]{:S(2)}) collective-permute-start(bf16[1,128,2048]{2,1,0:T(8,128)(2,1)S(1)} %copy.54), channel_id=1, source_target_pairs={{12,0},{16,4},{20,8},{24,12},{28,16},{32,20},{36,24},{40,28},{44,3... | collective-permute-start | bytes 1572872 | tf_op jit(solution)/shard_map/ppermute | solution.py:36
  484.5 3.0 copy-start.12
  487.4 0.8 copy-start.13
  489.8 1.0 copy-start.5
  490.3 228.7 %copy-start.6 = (f32[8,128,16]{1,2,0:T(8,128)S(1)}, f32[8,128,16]{1,2,0:T(8,128)}, u32[]{:S(2)}) copy-start(f32[8,128,16]{1,2,0:T(8,128)} %get-tuple-element.140) | copy-start | bytes 196612
  490.3 228.7 %copy-start.11 = (f32[8,128]{1,0:T(8,128)S(1)}, f32[8,128]{1,0:T(8,128)}, u32[]{:S(2)}) copy-start(f32[8,128]{1,0:T(8,128)} %get-tuple-element.139) | copy-start | bytes 12292
  490.8 228.9 %copy-start.4 = (bf16[1,128,1,1024]{1,3,2,0:T(8,128)(2,1)S(1)}, bf16[1,128,1,1024]{1,3,2,0:T(8,128)(2,1)}, u32[]{:S(2)}) copy-start(bf16[1,128,1,1024]{1,3,2,0:T(8,128)(2,1)} %copy-done.3) | copy-start | bytes 786436
  490.8 228.9 %copy-start.9 = (f32[8,128,16]{1,2,0:T(8,128)S(1)}, f32[8,128,16]{1,2,0:T(8,128)}, u32[]{:S(2)}) copy-start(f32[8,128,16]{1,2,0:T(8,128)} %copy-done.8) | copy-start | bytes 196612
  490.8 228.9 %copy-start.10 = (pred[128,128]{1,0:T(8,128)(4,1)S(1)}, pred[128,128]{1,0:T(8,128)(4,1)}, u32[]{:S(2)}) copy-start(pred[128,128]{1,0:T(8,128)(4,1)} %iota_compare_fusion) | copy-start | bytes 49156
  490.8 228.9 %copy-start.18 = (f32[8,128]{1,0:T(8,128)S(1)}, f32[8,128]{1,0:T(8,128)}, u32[]{:S(2)}) copy-start(f32[8,128]{1,0:T(8,128)} %copy-done.17) | copy-start | bytes 12292
  491.0 229.2 %copy-start.14 = (f32[1024]{0:T(1024)S(1)}, f32[1024]{0:T(1024)}, u32[]{:S(2)}) copy-start(f32[1024]{0:T(1024)} %param.11) | copy-start | bytes 12292
  491.3 230.0 %copy-start.1 = (bf16[1,128,2048]{2,1,0:T(8,128)(2,1)S(1)}, bf16[1,128,2048]{2,1,0:T(8,128)(2,1)}, u32[]{:S(2)}) copy-start(bf16[1,128,2048]{2,1,0:T(8,128)(2,1)} %param.8) | copy-start | bytes 1572868
Sparse Core Ops, SparseCore 0:
  173.4 195.4 all-reduce.3
  372.0 140.7 all-gather.3
